TPU v7x, 256 devices: a whole 4x4x8 slice. The times are simulated.
256 devices in a mesh: band: 32 (over y_lo, z, core), col: 8 (over x, y_hi).
Axes of the slice: x: 4, y: 4 (y_hi: 2, y_lo: 2; y = y_hi * 2 + y_lo), z: 8, core: 2. Of those that a mesh axis runs over, the one named last changes fastest.
Arguments:
- grad: float32 [16384, 8192], P('band', 'col'), as said below
Outputs:
- update: float32 [16384, 8192], P('band', 'col')
Inputs may be any that keep to these rules, and one draw needn't show every extreme that they name: `grad`: Real-valued gradient entries.
All inputs are finite; a program needn't handle non-finite values.
Results may differ from a plain program's by a relative error of at most 0.0003.
Values sent between devices are 32-bit elements; how exact they have to be, the bound alone decides.
No kernel may reach another device: no remote copies, remote signals or barrier semaphores. Data moves between devices by JAX's collectives and lax.ppermute only.
A program may use at most 64 MiB of HBM per device.

v0:
```python
import jax
import jax.numpy as jnp
from jax import lax
from jax.sharding import PartitionSpec as P

damping = 0.1


def passed_along(block, axis, distance):
    devices = range(lax.axis_size(axis))
    route = [(i - distance, i) for i in devices if i - distance in devices]
    return lax.ppermute(block, axis, route)


def gram(left, right):
    return lax.dot_general(left, right, (((1,), (1,)), ((), ())), precision=lax.Precision.HIGHEST)


def matmul(left, right):
    return jnp.dot(left, right, precision=lax.Precision.HIGHEST)


def cho_apply(matrix, rhs):
    factor = jnp.linalg.cholesky(matrix)
    half = lax.linalg.triangular_solve(factor, rhs, left_side=True, lower=True)
    return lax.linalg.triangular_solve(factor, half, left_side=True, lower=True, transpose_a=True)


def local(grad):
    band_rows = grad.shape[0]
    total_cols = grad.shape[1] * lax.axis_size("col")
    eye = jnp.eye(band_rows, dtype=jnp.float32)
    below = passed_along(grad, "band", 1)
    own_sum, cross_sum = lax.psum((gram(grad, grad), gram(below, grad)), "col")
    stat = own_sum / total_cols
    previous = passed_along(stat, "band", 1) + damping * eye
    own = stat + damping * eye
    cross = cross_sum / total_cols
    coupling = cho_apply(previous, cross)
    schur = own - matmul(cross.T, coupling)
    lowered = grad - matmul(coupling.T, below)
    solved = cho_apply(schur, lowered)
    next_coupling, next_solved = passed_along((coupling, solved), "band", -1)
    tail = matmul(next_coupling, next_solved)
    return solved - tail


def solution(mesh):
    return jax.shard_map(
        local,
        mesh=mesh,
        in_specs=(P("band", "col"),),
        out_specs=P("band", "col"),
        check_vma=False,
    )
```

profile of v0, /device:TPU:97, one launch (start us, length us, event | category | flops | bytes accessed | tf_op | source)
XLA Modules:
  0.0 577.3 jit_solution(15303351225335798192)
XLA Ops:
  6.5 5.4 collective-permute-start
  12.0 6.8 %fusion.119 = f32[512,512]{0,1:T(8,128)} fusion(f32[512,1024]{1,0:T(8,128)} %param.2), kind=kOutput, calls=%fused_computation.192 | convolution fusion | flops 3221225472 | bytes 3145728 | tf_op jit(solution)/shard_map/dot_general | solution.py:16
  18.7 16.5 %collective-permute-done = f32[512,1024]{1,0:T(8,128)S(1)} collective-permute-done((f32[512,1024]{1,0:T(8,128)}, f32[512,1024]{1,0:T(8,128)S(1)}, u32[]{:S(2)}, u32[]{:S(2)}) %collective-permute-start) | collective-permute-done | bytes 2097184 | tf_op jit(solution)/shard_map/ppermute | solution.py:12
  36.6 4.5 fusion.120
  41.1 115.9 %all-reduce.4.cloned.1.call-done = (f32[512,512]{0,1:T(8,128)}, f32[512,512]{0,1:T(8,128)}) async-done(((f32[512,512]{0,1:T(8,128)}, f32[512,512]{0,1:T(8,128)}), (f32[512,512]{0,1:T(8,128)}, f32[512,512]{0,1:T(8,128)})) %all-reduce.4.cloned.1.call-update) | async-done | bytes 2097168 | tf_op jit(solution)/shard_map/psum | solution.py:34
  157.0 2.3 broadcast_multiply_fusion.1
  159.3 8.7 %collective-permute-start.1 = (f32[512,512]{0,1:T(8,128)}, f32[512,512]{0,1:T(8,128)S(1)}, u32[]{:S(2)}, u32[]{:S(2)}) collective-permute-start(f32[512,512]{0,1:T(8,128)} %broadcast_multiply_fusion.1), channel_id=1, source_target_pairs={{0,8},{8,16},{16,24},{24,32},{32,40},{40,48},{48,56},{56,64},{64,7... | collective-permute-start | bytes 3145736 | tf_op jit(solution)/shard_map/ppermute | solution.py:12
  168.0 2.3 broadcast_multiply_fusion
  170.3 9.5 %collective-permute-done.1 = f32[512,512]{0,1:T(8,128)S(1)} collective-permute-done((f32[512,512]{0,1:T(8,128)}, f32[512,512]{0,1:T(8,128)S(1)}, u32[]{:S(2)}, u32[]{:S(2)}) %collective-permute-start.1) | collective-permute-done | bytes 1048608 | tf_op jit(solution)/shard_map/ppermute | solution.py:12
  180.9 2.5 copy.4
  185.9 11.7 %cholesky.286 = f32[128,128]{1,0:T(8,128)S(1)} custom-call(f32[128,128]{1,0:T(8,128)S(1)} %cholesky.426), custom_call_target="Cholesky" | custom-call | tf_op jit(solution)/shard_map/jit(cholesky)/cholesky | solution.py:24
  197.6 9.8 %custom-call.35 = f32[1,128,128]{1,2,0:T(8,128)S(1)} custom-call(f32[1,128,128]{2,1,0:T(8,128)S(1)} %get-tuple-element.63), custom_call_target="InvertDiagBlocksLowerTriangular" | custom-call | tf_op jit(solution)/shard_map/jit(cholesky)/cholesky | solution.py:24
  210.8 11.7 %cholesky.305 = f32[128,128]{1,0:T(8,128)S(1)} custom-call(f32[128,128]{1,0:T(8,128)S(1)} %cholesky.430), custom_call_target="Cholesky" | custom-call | tf_op jit(solution)/shard_map/jit(cholesky)/cholesky | solution.py:24
  223.3 10.9 %custom-call.36 = f32[1,128,128]{1,2,0:T(8,128)} custom-call(f32[1,128,128]{2,1,0:T(8,128)S(1)} %get-tuple-element.61), custom_call_target="InvertDiagBlocksLowerTriangular" | custom-call | tf_op jit(solution)/shard_map/jit(cholesky)/cholesky | solution.py:24
  237.2 1.5 slice_subtract_fusion.13
  238.7 11.7 %cholesky.326 = f32[128,128]{1,0:T(8,128)S(1)} custom-call(f32[128,128]{1,0:T(8,128)S(1)} %cholesky.435), custom_call_target="Cholesky" | custom-call | tf_op jit(solution)/shard_map/jit(cholesky)/cholesky | solution.py:24
  250.5 9.8 %custom-call.37 = f32[1,128,128]{1,2,0:T(8,128)S(1)} custom-call(f32[1,128,128]{2,1,0:T(8,128)S(1)} %get-tuple-element.59), custom_call_target="InvertDiagBlocksLowerTriangular" | custom-call | tf_op jit(solution)/shard_map/jit(cholesky)/cholesky | solution.py:24
  262.0 11.9 %cholesky.343 = f32[128,128]{1,0:T(8,128)S(1)} custom-call(f32[128,128]{1,0:T(8,128)S(1)} %slice_subtract_fusion.14), custom_call_target="Cholesky" | custom-call | tf_op jit(solution)/shard_map/jit(cholesky)/cholesky | solution.py:24
  280.2 14.6 %while.2 = (s32[]{:T(128)}, f32[512,512]{0,1:T(8,128)}, s32[4,2]{0,1:T(2,128)S(1)}, f32[4,128,128]{2,1,0:T(8,128)}, s32[]{:T(128)}) while((s32[]{:T(128)}, f32[512,512]{0,1:T(8,128)}, s32[4,2]{0,1:T(2,128)S(1)}, f32[4,128,128]{2,1,0:T(8,128)}, s32[]{:T(128)}) %tuple.43), condition=%wide.while_cond, body=%wide.while_body.sunk | while | flops 2 | bytes 393829 | solution.py:26
  280.9 2.3 dynamic-slice.13
  284.6 2.3 dynamic-slice.13
  288.2 2.3 dynamic-slice.13
  291.9 2.2 dynamic-slice.13
  294.8 40.2 %custom-call.30 = f32[4,128,128]{1,2,0:T(8,128)S(1)} custom-call(f32[4,128,128]{2,1,0:T(8,128)} %get-tuple-element.13), custom_call_target="InvertDiagBlocksLowerTriangular" | custom-call | tf_op jit(solution)/shard_map/triangular_solve | solution.py:26
  335.0 1.5 fusion.51
  340.8 1.5 fusion.24
  348.3 2.0 convolution_subtract_fusion.2
  354.1 12.1 %cholesky.358 = f32[128,128]{1,0:T(8,128)S(1)} custom-call(f32[128,128]{1,0:T(8,128)S(1)} %cholesky.439), custom_call_target="Cholesky" | custom-call | tf_op jit(solution)/shard_map/jit(cholesky)/cholesky | solution.py:24
  366.2 9.8 %custom-call.38 = f32[1,128,128]{1,2,0:T(8,128)S(1)} custom-call(f32[1,128,128]{2,1,0:T(8,128)S(1)} %get-tuple-element.57), custom_call_target="InvertDiagBlocksLowerTriangular" | custom-call | tf_op jit(solution)/shard_map/jit(cholesky)/cholesky | solution.py:24
  379.2 11.7 %cholesky.377 = f32[128,128]{1,0:T(8,128)S(1)} custom-call(f32[128,128]{1,0:T(8,128)S(1)} %cholesky.443), custom_call_target="Cholesky" | custom-call | tf_op jit(solution)/shard_map/jit(cholesky)/cholesky | solution.py:24
  392.0 10.4 %custom-call.39 = f32[1,128,128]{1,2,0:T(8,128)} custom-call(f32[1,128,128]{2,1,0:T(8,128)S(1)} %get-tuple-element.55), custom_call_target="InvertDiagBlocksLowerTriangular" | custom-call | tf_op jit(solution)/shard_map/jit(cholesky)/cholesky | solution.py:24
  404.7 1.5 convolution_subtract_fusion.9
  406.8 13.3 %cholesky.398 = f32[128,128]{1,0:T(8,128)} custom-call(f32[128,128]{1,0:T(8,128)} %cholesky.448), custom_call_target="Cholesky" | custom-call | tf_op jit(solution)/shard_map/jit(cholesky)/cholesky | solution.py:24
  420.2 1.5 select_reduce_fusion.1
  421.7 1.6 copy.19
  424.1 11.3 %custom-call.40 = f32[1,128,128]{1,2,0:T(8,128)} custom-call(f32[1,128,128]{2,1,0:T(8,128)} %get-tuple-element.53), custom_call_target="InvertDiagBlocksLowerTriangular" | custom-call | tf_op jit(solution)/shard_map/jit(cholesky)/cholesky | solution.py:24
  437.8 11.7 %cholesky.415 = f32[128,128]{1,0:T(8,128)S(1)} custom-call(f32[128,128]{1,0:T(8,128)S(1)} %convolution_subtract_fusion.10), custom_call_target="Cholesky" | custom-call | tf_op jit(solution)/shard_map/jit(cholesky)/cholesky | solution.py:24
  457.2 12.2 %while.3 = (s32[]{:T(128)}, f32[512,512]{0,1:T(8,128)}, s32[4,2]{0,1:T(2,128)S(1)}, f32[4,128,128]{2,1,0:T(8,128)S(1)}, s32[]{:T(128)}) while((s32[]{:T(128)}, f32[512,512]{0,1:T(8,128)}, s32[4,2]{0,1:T(2,128)S(1)}, f32[4,128,128]{2,1,0:T(8,128)S(1)}, s32[]{:T(128)}) %tuple.52), condition=%wide.while_cond.1, body=%wide.while_body.1.sunk | while | flops 2 | bytes 393321 | solution.py:26
  457.9 2.2 dynamic-slice.15
  461.0 2.2 dynamic-slice.15
  464.0 2.2 dynamic-slice.15
  467.1 2.2 dynamic-slice.15
  469.4 39.5 %custom-call.31 = f32[4,128,128]{1,2,0:T(8,128)S(1)} custom-call(f32[4,128,128]{2,1,0:T(8,128)S(1)} %get-tuple-element.21), custom_call_target="InvertDiagBlocksLowerTriangular" | custom-call | tf_op jit(solution)/shard_map/triangular_solve | solution.py:26
  508.9 5.3 convolution_subtract_fusion.1
  524.6 1.9 collective-permute-start.3
  526.7 1.9 collective-permute-start.2
  528.6 36.5 %collective-permute-done.2 = f32[512,512]{1,0:T(8,128)S(1)} collective-permute-done((f32[512,512]{1,0:T(8,128)S(1)}, f32[512,512]{1,0:T(8,128)S(1)}, u32[]{:S(2)}, u32[]{:S(2)}) %collective-permute-start.2) | collective-permute-done | bytes 1048608 | tf_op jit(solution)/shard_map/ppermute | solution.py:12
  565.1 4.9 convolution_subtract_fusion
  (158 shorter events, 66.2 us)
Async XLA Ops:
  6.5 30.0 %copy-start = (f32[512,1024]{1,0:T(8,128)S(1)}, f32[512,1024]{1,0:T(8,128)}, u32[]{:S(2)}) copy-start(f32[512,1024]{1,0:T(8,128)} %param.2) | copy-start | bytes 6291460
  6.5 150.5 %all-reduce.4.cloned.1.call-start = ((), (), s32[]{:S(2)}) async-start(), calls=%async_computation | async-start | bytes 4194304 | tf_op jit(solution)/shard_map/psum | solution.py:34
  6.5 28.7 %collective-permute-start = (f32[512,1024]{1,0:T(8,128)}, f32[512,1024]{1,0:T(8,128)S(1)}, u32[]{:S(2)}, u32[]{:S(2)}) collective-permute-start(f32[512,1024]{1,0:T(8,128)} %param.2), channel_id=1, source_target_pairs={{0,8},{8,16},{16,24},{24,32},{32,40},{40,48},{48,56},{56,64},{64,7... | collective-permute-start | bytes 6291464 | tf_op jit(solution)/shard_map/ppermute | solution.py:12
  35.3 1.3 copy-start.1
  159.3 20.5 %collective-permute-start.1 = (f32[512,512]{0,1:T(8,128)}, f32[512,512]{0,1:T(8,128)S(1)}, u32[]{:S(2)}, u32[]{:S(2)}) collective-permute-start(f32[512,512]{0,1:T(8,128)} %broadcast_multiply_fusion.1), channel_id=1, source_target_pairs={{0,8},{8,16},{16,24},{24,32},{32,40},{40,48},{48,56},{56,64},{64,7... | collective-permute-start | bytes 3145736 | tf_op jit(solution)/shard_map/ppermute | solution.py:12
  184.9 1.0 copy-start.9
  294.8 44.5 %copy-start.4 = (f32[512,512]{0,1:T(8,128)S(1)}, f32[512,512]{0,1:T(8,128)}, u32[]{:S(2)}) copy-start(f32[512,512]{0,1:T(8,128)} %get-tuple-element.160) | copy-start | bytes 3145732
  335.0 7.3 %copy-start.15 = (f32[4,128,128]{1,2,0:T(8,128)}, f32[4,128,128]{1,2,0:T(8,128)S(1)}, u32[]{:S(2)}) copy-start(f32[4,128,128]{1,2,0:T(8,128)S(1)} %custom-call.30) | copy-start | bytes 786436
  335.0 5.3 copy-start.6
  342.7 3.5 copy-start.16
  344.4 3.9 copy-start.13
  344.4 3.9 copy-start.14
  345.8 1.8 copy-start.2
  346.6 1.0 copy-start.7
  347.6 0.7 copy-start.11
  353.1 1.0 copy-start.10
  378.5 0.7 copy-start.17
  457.2 51.7 %copy-start.3 = (f32[128,512]{1,0:T(8,128)S(1)}, f32[128,512]{1,0:T(8,128)}, u32[]{:S(2)}) copy-start(f32[128,512]{1,0:T(8,128)} %copy-done.2) | copy-start | bytes 786436
  457.2 51.7 %copy-start.8 = (f32[128,512]{1,0:T(8,128)S(1)}, f32[128,512]{1,0:T(8,128)}, u32[]{:S(2)}) copy-start(f32[128,512]{1,0:T(8,128)} %copy-done.7) | copy-start | bytes 786436
  508.9 6.0 %copy-start.5 = (f32[512,512]{0,1:T(8,128)S(1)}, f32[512,512]{0,1:T(8,128)}, u32[]{:S(2)}) copy-start(f32[512,512]{0,1:T(8,128)} %get-tuple-element.161) | copy-start | bytes 3145732
  524.4 2.2 copy-start.12
  524.6 40.5 %collective-permute-start.3 = (f32[512,1024]{1,0:T(8,128)S(1)}, f32[512,1024]{1,0:T(8,128)S(1)}, u32[]{:S(2)}, u32[]{:S(2)}) collective-permute-start(f32[512,1024]{1,0:T(8,128)S(1)} %pad_maximum_fusion), channel_id=1, source_target_pairs={{8,0},{16,8},{24,16},{32,24},{40,32},{48,40},{56,48},{64,56},{72,6... | collective-permute-start | bytes 6291464 | tf_op jit(solution)/shard_map/ppermute | solution.py:12
  526.7 38.4 %collective-permute-start.2 = (f32[512,512]{1,0:T(8,128)S(1)}, f32[512,512]{1,0:T(8,128)S(1)}, u32[]{:S(2)}, u32[]{:S(2)}) collective-permute-start(f32[512,512]{1,0:T(8,128)S(1)} %pad_maximum_fusion.1), channel_id=1, source_target_pairs={{8,0},{16,8},{24,16},{32,24},{40,32},{48,40},{56,48},{64,56},{72,6... | collective-permute-start | bytes 3145736 | tf_op jit(solution)/shard_map/ppermute | solution.py:12
Sparse Core Ops, SparseCore 0:
  41.2 115.7 all-reduce.3
where the time goes:
time: 585 us; the launch traced here: 577 us
  other arithmetic  256 us (44%)
  waiting for transfers between devices  178 us (30%)
  matrix products  60.2 us (10%)
  local copies, waits for them, and re-layouts  44.6 us (8%)
  between operations  19.5 us (3%)
  starting transfers between devices  17.9 us (3%)
    another operation x29, other arithmetic, cho_apply(): factor = jnp.linalg.cholesky(matrix)  165 us
    psum x1, waiting for transfers between devices, local(): own_sum, cross_sum = lax.psum((gram(grad, grad), gram(below, grad)), 'col')  116 us
    another operation x7, other arithmetic, cho_apply(): lax.linalg.triangular_solve(factor, half, left_side=True, lower=True, tra...  82.3 us
    ppermute x4, waiting for transfers between devices, passed_along(): return lax.ppermute(block, axis, route)  62.5 us
    another operation x40, local copies, waits for them, and re-layouts  26.5 us
    ppermute x4, starting transfers between devices, passed_along(): return lax.ppermute(block, axis, route)  17.9 us
    another operation x12, matrix products, cho_apply(): factor = jnp.linalg.cholesky(matrix)  14.4 us
    another operation x14, matrix products, cho_apply(): half = lax.linalg.triangular_solve(factor, rhs, left_side=True, lower=True)  12.7 us
  transfers between devices with their start and end apart: 5, of which 4 were waited for; matrix products, arithmetic and copies ran while one was open for 2% of the time, Pallas kernels for 0%

commit v1 on v0

v1 whole, which is shorter than its diff:
```python
import jax
import jax.numpy as jnp
from jax import lax
from jax.experimental import pallas as pl
from jax.experimental.pallas import tpu as pltpu
from jax.sharding import PartitionSpec as P

f32, bf16 = jnp.float32, jnp.bfloat16
damping = 0.1
NN = (((1,), (0,)), ((), ()))
NT = (((1,), (1,)), ((), ()))


def dot1(left, right, dims=NN):
    return lax.dot_general(left, right, dims, preferred_element_type=f32)


def split(a):
    high = a.astype(bf16)
    return high, (a - high.astype(f32)).astype(bf16)


def dot3(left, right, dims=NN):
    (lh, ll), (rh, rl) = left, right
    return dot1(lh, rh, dims) + (dot1(lh, rl, dims) + dot1(ll, rh, dims))


def dot6(left, right, dims=NN):
    return lax.dot_general(
        left, right, dims, precision=lax.Precision.HIGHEST, preferred_element_type=f32
    )


def diagonal(n):
    rows = lax.broadcasted_iota(jnp.int32, (n, n), 0)
    return rows == lax.broadcasted_iota(jnp.int32, (n, n), 1)


def sweep_all(w_ref):
    n = w_ref.shape[0]
    lane = lax.broadcasted_iota(jnp.int32, (n, n), 1)
    sub = lax.broadcasted_iota(jnp.int32, (n, n), 0)
    along = lax.broadcasted_iota(jnp.int32, (1, n), 1)

    def sweep(j, carry):
        w = w_ref[...]
        row = w_ref[pl.ds(j, 1), :]
        col = jnp.sum(jnp.where(lane == j, w, 0.0), axis=1, keepdims=True)
        pivot = jnp.sum(jnp.where(along == j, row, 0.0), axis=1, keepdims=True)
        inv = 1.0 / pivot
        new = w - col * (row * inv)
        new = jnp.where(sub == j, row * inv, new)
        new = jnp.where(lane == j, col * inv, new)
        w_ref[...] = jnp.where(jnp.logical_and(sub == j, lane == j), -inv, new)
        return carry

    lax.fori_loop(0, n, sweep, 0)


def invert(a_ref, x_ref, s_ref, e_ref):
    n = a_ref.shape[0]
    on = diagonal(n)
    a = a_ref[...]
    d = jnp.where(on, a, 0.0)
    s_row = lax.rsqrt(jnp.sum(d, axis=0, keepdims=True))
    s_col = lax.rsqrt(jnp.sum(d, axis=1, keepdims=True))
    s = a * s_col * s_row
    s_ref[...] = s
    high = s.astype(bf16)
    s2 = dot1(high, high)
    bound = jnp.sqrt(jnp.max(jnp.sum(jnp.abs(s2), axis=1, keepdims=True))) * 1.02
    alpha = 1.9 / bound
    e_ref[...] = jnp.where(on, 1.0, 0.0) - (2 * alpha) * s + (alpha * alpha) * s2
    x_ref[...] = jnp.where(on, 2 * alpha, 0.0) - (alpha * alpha) * s

    def unsettled(state):
        step, size = state
        return jnp.logical_and(step < 14, size > 0.1)

    def square(state):
        step, _ = state
        e = e_ref[...].astype(bf16)
        x = x_ref[...]
        x_ref[...] = x + dot1(x.astype(bf16), e)
        e = dot1(e, e)
        e_ref[...] = e
        return step + 1, jnp.sum(e * e)

    lax.while_loop(unsettled, square, (0, jnp.float32(1.0)))

    def rough(state):
        step, size = state
        return jnp.logical_and(step < 5, size > 1e-4)

    def refine(state):
        step, _ = state
        x = x_ref[...]
        r = jnp.where(on, 1.0, 0.0) - dot3(split(s_ref[...]), split(x))
        x_ref[...] = x + dot1(x.astype(bf16), r.astype(bf16))
        return step + 1, jnp.sum(r * r)

    lax.while_loop(rough, refine, (0, jnp.float32(1.0)))
    x = x_ref[...]
    r = jnp.where(on, 1.0, 0.0) - dot6(s_ref[...], x)
    x_ref[...] = (x + dot1(x.astype(bf16), r.astype(bf16))) * s_col * s_row

    @pl.when(jnp.logical_not(jnp.sum(r * r) < 1e-6))
    def _():
        s_ref[...] = a_ref[...]
        sweep_all(s_ref)
        x_ref[...] = -s_ref[...]


VMEM = pl.BlockSpec(memory_space=pltpu.VMEM)
PARAMS = pltpu.CompilerParams(vmem_limit_bytes=50 << 20)


def inverse(a):
    n = a.shape[0]
    return pl.pallas_call(
        invert,
        out_shape=jax.ShapeDtypeStruct((n, n), f32),
        in_specs=[VMEM],
        out_specs=VMEM,
        scratch_shapes=[pltpu.VMEM((n, n), f32)] * 2,
        compiler_params=PARAMS,
    )(a)


def solve_kernel(x_ref, ct_ref, h_ref, below_ref, above_ref, kt_ref, z_ref, a_ref, xs_ref, s_ref, e_ref):
    ct = split(ct_ref[...])
    kt_ref[...] = dot3(ct, split(x_ref[...]))
    kt = split(kt_ref[...])
    a_ref[...] = h_ref[...] - dot3(kt, ct, NT)
    invert(a_ref, xs_ref, s_ref, e_ref)
    y = above_ref[...] - dot3(kt, split(below_ref[...]))
    z_ref[...] = dot3(split(xs_ref[...]), split(y))


def solve(x, ct, h, below, above):
    n, m = above.shape
    return pl.pallas_call(
        solve_kernel,
        out_shape=[jax.ShapeDtypeStruct((n, n), f32), jax.ShapeDtypeStruct((n, m), f32)],
        in_specs=[VMEM] * 5,
        out_specs=[VMEM] * 2,
        scratch_shapes=[pltpu.VMEM((n, n), f32)] * 4,
        compiler_params=PARAMS,
    )(x, ct, h, below, above)


def handed(block, distance):
    n = lax.axis_size("band")
    return lax.ppermute(block, "band", [(i, (i + distance) % n) for i in range(n)])


def gram(left, right):
    return lax.dot_general(left, right, NT, precision=lax.Precision.HIGH)


def summed(part, scale):
    count = lax.axis_size("col")
    rows, cols = part.shape
    stripes = lax.all_to_all(part.reshape(count, rows // count, cols), "col", 0, 0)
    stripe = stripes.sum(0) * scale
    every = jnp.broadcast_to(stripe[None], stripes.shape)
    return lax.all_to_all(every, "col", 0, 0).reshape(rows, cols)


def local(grad):
    rows = grad.shape[0]
    total_cols = grad.shape[1] * lax.axis_size("col")
    band, bands = lax.axis_index("band"), lax.axis_size("band")
    above = handed(grad, -1)
    own = summed(gram(grad, grad), 1.0 / total_cols) + damping * jnp.eye(rows, dtype=f32)
    last = band == bands - 1
    cross_t = summed(gram(above, grad), jnp.where(last, 0.0, 1.0 / total_cols))
    own_above = handed(own, -1)
    kt, solved = solve(inverse(own), cross_t, own_above, grad, above)
    mine = handed(solved, 1)
    tail = lax.dot_general(kt, solved, (((0,), (0,)), ((), ())), precision=lax.Precision.HIGH)
    return mine - tail


def solution(mesh):
    return jax.shard_map(
        local,
        mesh=mesh,
        in_specs=(P("band", "col"),),
        out_specs=P("band", "col"),
        check_vma=False,
    )
```

time: 585 us -> 542 us (0.926)
  the two profiles are of different devices: /device:TPU:97 before, /device:TPU:16 now
where the time goes in v1:
time: 542 us; the launch traced here: 541 us
  waiting for transfers between devices  242 us (45%)
  Pallas kernels  219 us (40%)
  starting transfers between devices  46.1 us (9%)
  blocking collectives  17.4 us (3%)
  matrix products  11.9 us (2%)
    ppermute x3, waiting for transfers between devices, handed(): lax.ppermute(block, 'band', [(i, (i + distance) % n) for i in range(n)])  240 us
    pallas_call x1, Pallas kernels, inverse(): pl.pallas_call(invert, out_shape=jax.ShapeDtypeStruct((n, n), f32), in_sp...  201 us
    ppermute x3, starting transfers between devices, handed(): lax.ppermute(block, 'band', [(i, (i + distance) % n) for i in range(n)])  28 us
    pallas_call x1, Pallas kernels, solve(): pl.pallas_call(solve_kernel, out_shape=[jax.ShapeDtypeStruct((n, n), f32)...  18 us
    all_to_all x1, blocking collectives, summed(): lax.all_to_all(part.reshape(count, rows // count, cols), 'col', 0, 0)  17.4 us
    all_to_all x2, starting transfers between devices, summed(): return lax.all_to_all(every, 'col', 0, 0).reshape(rows, cols)  13 us
  transfers between devices with their start and end apart: 6, of which 3 were waited for; matrix products, arithmetic and copies ran while one was open for 3% of the time, Pallas kernels for 37%

profile of v1, /device:TPU:16, one launch (start us, length us, event | category | flops | bytes accessed | tf_op | source)
XLA Modules:
  0.0 541.4 jit_solution(12009194978899580370)
XLA Ops:
  0.0 6.0 %collective-permute-start = (f32[512,1024]{1,0:T(8,128)}, f32[512,1024]{1,0:T(8,128)}, u32[]{:S(2)}, u32[]{:S(2)}) collective-permute-start(f32[512,1024]{1,0:T(8,128)} %below_ref.1), channel_id=1, source_target_pairs={{0,248},{8,0},{16,8},{24,16},{32,24},{40,32},{48,40},{56,48},{64,5... | collective-permute-start | bytes 6291464 | tf_op jit(solution)/shard_map/ppermute | solution.py:154
  6.0 4.1 fusion
  10.1 17.4 %all_to_all.20 = f32[8,64,512]{2,1,0:T(8,128)S(1)} all-to-all(f32[8,64,512]{2,1,0:T(8,128)S(1)} %bitcast.12), channel_id=1, replica_groups=mesh['band'=32,'col'=8] {'col'}, dimensions={0} | all-to-all | bytes 2097152 | tf_op jit(solution)/shard_map/all_to_all | solution.py:164
  27.5 0.0 copy-start
  27.5 0.1 reduce_sum.18
  27.6 1.1 broadcast_in_dim.4
  28.7 5.8 %all-to-all-start.1 = ((f32[8,64,512]{2,1,0:T(8,128)}), f32[8,64,512]{2,1,0:T(8,128)S(1)}, u32[]{:S(2)}, u32[]{:S(2)}) async-start(f32[8,64,512]{2,1,0:T(8,128)} %broadcast_in_dim.4), calls=%async_computation.1 | async-start | bytes 2097152 | tf_op jit(solution)/shard_map/all_to_all | solution.py:167
  34.5 3.9 collective-permute-done.above_ref
  38.4 0.0 copy-done
  38.4 4.4 fusion.1
  42.8 2.5 all-to-all-done.1
  45.3 5.1 all-to-all-start.2
  50.4 0.1 bitcast_add_fusion.a_ref
  50.4 22.0 %collective-permute-start.1 = (f32[512,512]{1,0:T(8,128)S(1)}, f32[512,512]{1,0:T(8,128)}, u32[]{:S(2)}, u32[]{:S(2)}) collective-permute-start(f32[512,512]{1,0:T(8,128)S(1)} %bitcast_add_fusion.a_ref), channel_id=1, source_target_pairs={{0,248},{8,0},{16,8},{24,16},{32,24},{40,32},{48,40},{56,48},{64,5... | collective-permute-start | bytes 3145736 | tf_op jit(solution)/shard_map/ppermute | solution.py:154
  72.5 0.0 all-to-all-done.2
  72.5 0.1 reduce_sum.19
  72.6 1.1 broadcast_in_dim.5
  73.7 7.2 %all-to-all-start.3 = ((f32[8,64,512]{2,1,0:T(8,128)}), f32[8,64,512]{2,1,0:T(8,128)S(1)}, u32[]{:S(2)}, u32[]{:S(2)}) async-start(f32[8,64,512]{2,1,0:T(8,128)} %broadcast_in_dim.5), calls=%async_computation.3 | async-start | bytes 2097152 | tf_op jit(solution)/shard_map/all_to_all | solution.py:167
  80.9 201.3 %shard_map.17.x_ref = f32[512,512]{1,0:T(8,128)S(1)} custom-call(f32[512,512]{1,0:T(8,128)S(1)} %bitcast_add_fusion.a_ref), custom_call_target="tpu_custom_call" | custom-call | tf_op jit(solution)/shard_map/pallas_call | solution.py:120
  282.2 0.0 collective-permute-done.1.h_ref
  282.2 0.0 all-to-all-done.3
  282.2 18.0 %shard_map.18 = (f32[512,512]{1,0:T(8,128)S(1)}, f32[512,1024]{1,0:T(8,128)}) custom-call(f32[512,512]{1,0:T(8,128)S(1)} %shard_map.17.x_ref, f32[512,512]{1,0:T(8,128)S(1)} %bitcast.11, f32[512,512]{1,0:T(8,128)} %collective-permute-done.1.h_ref, f32[512,1024]{1,0:T(8,128)} %below_ref.1, f32[512,1024]{1,0:T(8,128)} %collective-permute-done.above_ref), custom_call_target="tpu_custom_call" | custom-call | tf_op jit(solution)/shard_map/pallas_call | solution.py:142
  300.2 0.0 collective-permute-start.2
  300.2 3.5 fusion.2
  303.7 236.0 %collective-permute-done.2 = f32[512,1024]{1,0:T(8,128)S(1)} collective-permute-done((f32[512,1024]{1,0:T(8,128)}, f32[512,1024]{1,0:T(8,128)S(1)}, u32[]{:S(2)}, u32[]{:S(2)}) %collective-permute-start.2) | collective-permute-done | bytes 2097184 | tf_op jit(solution)/shard_map/ppermute | solution.py:154
  539.7 1.7 sub.3
  (2 shorter events, 0.0 us)
Async XLA Ops:
  0.0 38.4 %collective-permute-start = (f32[512,1024]{1,0:T(8,128)}, f32[512,1024]{1,0:T(8,128)}, u32[]{:S(2)}, u32[]{:S(2)}) collective-permute-start(f32[512,1024]{1,0:T(8,128)} %below_ref.1), channel_id=1, source_target_pairs={{0,248},{8,0},{16,8},{24,16},{32,24},{40,32},{48,40},{56,48},{64,5... | collective-permute-start | bytes 6291464 | tf_op jit(solution)/shard_map/ppermute | solution.py:154
  27.5 10.9 %copy-start = (f32[512,1024]{1,0:T(8,128)S(1)}, f32[512,1024]{1,0:T(8,128)}, u32[]{:S(2)}) copy-start(f32[512,1024]{1,0:T(8,128)} %below_ref.1) | copy-start | bytes 6291460
  28.7 16.6 %all-to-all-start.1 = ((f32[8,64,512]{2,1,0:T(8,128)}), f32[8,64,512]{2,1,0:T(8,128)S(1)}, u32[]{:S(2)}, u32[]{:S(2)}) async-start(f32[8,64,512]{2,1,0:T(8,128)} %broadcast_in_dim.4), calls=%async_computation.1 | async-start | bytes 2097152 | tf_op jit(solution)/shard_map/all_to_all | solution.py:167
  45.3 27.2 %all-to-all-start.2 = ((f32[8,64,512]{2,1,0:T(8,128)}), f32[8,64,512]{2,1,0:T(8,128)S(1)}, u32[]{:S(2)}, u32[]{:S(2)}) async-start(f32[8,64,512]{2,1,0:T(8,128)} %bitcast.2), calls=%async_computation.2 | async-start | bytes 2097152 | tf_op jit(solution)/shard_map/all_to_all | solution.py:164
  50.4 231.8 %collective-permute-start.1 = (f32[512,512]{1,0:T(8,128)S(1)}, f32[512,512]{1,0:T(8,128)}, u32[]{:S(2)}, u32[]{:S(2)}) collective-permute-start(f32[512,512]{1,0:T(8,128)S(1)} %bitcast_add_fusion.a_ref), channel_id=1, source_target_pairs={{0,248},{8,0},{16,8},{24,16},{32,24},{40,32},{48,40},{56,48},{64,5... | collective-permute-start | bytes 3145736 | tf_op jit(solution)/shard_map/ppermute | solution.py:154
  73.7 208.5 %all-to-all-start.3 = ((f32[8,64,512]{2,1,0:T(8,128)}), f32[8,64,512]{2,1,0:T(8,128)S(1)}, u32[]{:S(2)}, u32[]{:S(2)}) async-start(f32[8,64,512]{2,1,0:T(8,128)} %broadcast_in_dim.5), calls=%async_computation.3 | async-start | bytes 2097152 | tf_op jit(solution)/shard_map/all_to_all | solution.py:167
  300.2 239.5 %collective-permute-start.2 = (f32[512,1024]{1,0:T(8,128)}, f32[512,1024]{1,0:T(8,128)S(1)}, u32[]{:S(2)}, u32[]{:S(2)}) collective-permute-start(f32[512,1024]{1,0:T(8,128)} %get-tuple-element.7), channel_id=1, source_target_pairs={{0,8},{8,16},{16,24},{24,32},{32,40},{40,48},{48,56},{56,64},{64,7... | collective-permute-start | bytes 6291464 | tf_op jit(solution)/shard_map/ppermute | solution.py:154
